TPU v7x, 32 devices: a whole 2x2x4 slice. The times are simulated.
32 devices in a mesh: gx: 4 (over y, core), gy: 8 (over z, x).
Axes of the slice: x: 2, y: 2, z: 4, core: 2. Of those that a mesh axis runs over, the one named last changes fastest.
Arguments:
- displacement: float32 [512, 4096], P('gx', 'gy'), may hold values from -4.2 to 4.2
- velocity: float32 [512, 4096], P('gx', 'gy'), may hold values from -3 to 3
- load: float32 [512, 4096], P('gx', 'gy'), may hold values from -38 to 38
Outputs:
- new_displacement: float32 [512, 4096], P('gx', 'gy')
All inputs are finite; a program needn't handle non-finite values.
Results may differ from a plain program's by a relative error of at most 0.000031.
Values sent between devices are 32-bit elements; how exact they have to be, the bound alone decides.
A program may use at most 64 MiB of HBM per device.

v0:
```python
import jax
import jax.numpy as jnp
from jax import lax
from jax.sharding import PartitionSpec as P

COARSE = 3


mass_term = 0.0001
damping = 0.5
tension_base = 1.0
tension_gain = 3.0


def extended(shard, sides, width):
    for axis, dim in sides:
        peers, length = (lax.axis_size(axis), shard.shape[dim])
        up = [(i, (i + 1) % peers) for i in range(peers - 1)]
        down = [(j, i) for i, j in up]
        last = lax.slice_in_dim(shard, length - width, length, axis=dim)
        leading = lax.slice_in_dim(shard, 0, width, axis=dim)
        before = lax.ppermute(last, axis, up)
        after = lax.ppermute(leading, axis, down)
        shard = jnp.concatenate([before, shard, after], axis=dim)
    return shard


def shifted(value, axis, steps):
    count = lax.axis_size(axis)
    leading, last = (max(0, -steps), min(count, count - steps))
    return lax.ppermute(value, axis, [(source, source + steps) for source in range(leading, last)])


def stencil(padded):
    centre = padded[2:-2, 2:-2]
    near_sum = padded[1:-3, 2:-2] + padded[3:-1, 2:-2] + padded[2:-2, 1:-3] + padded[2:-2, 3:-1]
    diag_sum = padded[1:-3, 1:-3] + padded[1:-3, 3:-1] + padded[3:-1, 1:-3] + padded[3:-1, 3:-1]
    far_sum = padded[:-4, 2:-2] + padded[4:, 2:-2] + padded[2:-2, :-4] + padded[2:-2, 4:]
    laplace = 4.0 * centre - near_sum
    biharm = 20.0 * centre - 8.0 * near_sum + 2.0 * diag_sum + far_sum
    return (centre, biharm, laplace)


def operate(padded, level, tension):
    centre, biharm, laplace = stencil(padded)
    return mass_term * centre + biharm / 16.0**level + tension * laplace / 4.0**level


def diagonal(level, tension):
    return mass_term + 20.0 / 16.0**level + 4.0 * tension / 4.0**level


def restrict(field):
    height, breadth = field.shape
    return 0.25 * field.reshape(height // 2, 2, breadth // 2, 2).sum(axis=(1, 3))


def prolong(field):
    return jnp.repeat(jnp.repeat(field, 2, axis=0), 2, axis=1)


def pad_fine(field):
    return extended(field, (("gx", 0), ("gy", 1)), 2)


def move_rows(field, offset):
    return shifted(field, "gx", offset)


def move_cols(field, offset):
    return shifted(field, "gy", offset)


def pad_owner(field):
    stacked = jnp.concatenate([move_rows(field[-2:], 4), field, move_rows(field[:2], -4)], 0)
    return jnp.concatenate(
        [move_cols(stacked[:, -2:], 4), stacked, move_cols(stacked[:, :2], -4)], 1
    )


def collect(block):
    rows_held = jnp.concatenate([block] + [move_rows(block, -stride) for stride in (1, 2, 3)], 0)
    whole = jnp.concatenate(
        [rows_held] + [move_cols(rows_held, -stride) for stride in (1, 2, 3)], 1
    )
    return whole


def distribute(whole):
    height = whole.shape[0] // 4
    breadth = whole.shape[1] // 4
    row_offset = lax.axis_index("gx") % 4
    col_offset = lax.axis_index("gy") % 4
    rows_held = whole[:height]
    for stride in (1, 2, 3):
        arrived = move_rows(whole[stride * height : (stride + 1) * height], stride)
        rows_held = jnp.where(row_offset == stride, arrived, rows_held)
    result = rows_held[:, :breadth]
    for stride in (1, 2, 3):
        arrived = move_cols(rows_held[:, stride * breadth : (stride + 1) * breadth], stride)
        result = jnp.where(col_offset == stride, arrived, result)
    return result


def descend(rhs_field, level, tension, coarse_pad):
    padder = pad_fine if level < 2 else coarse_pad
    weight = damping / diagonal(level, tension)
    update = weight * rhs_field
    if level == 3:
        for counter in range(COARSE - 1):
            update = update + weight * (rhs_field - operate(padder(update), level, tension))
        return update
    leftover = rhs_field - operate(padder(update), level, tension)
    lower = restrict(leftover)
    if level == 1:
        correction = distribute(descend(collect(lower), 2, tension, pad_owner))
    else:
        correction = descend(lower, level + 1, tension, coarse_pad)
    update = update + prolong(correction)
    return update + weight * (rhs_field - operate(padder(update), level, tension))


def global_energy(padded, predicted):
    down_diff = padded[3:-1, 2:-2] - predicted
    right_diff = padded[2:-2, 3:-1] - predicted
    return lax.psum(jnp.sum(down_diff * down_diff + right_diff * right_diff), ("gx", "gy"))


def body(displacement, velocity, load):
    height, breadth = displacement.shape
    cells_total = height * lax.axis_size("gx") * breadth * lax.axis_size("gy")
    predicted = displacement + velocity
    padded = pad_fine(predicted)
    energy = global_energy(padded, predicted)
    tension = tension_base + tension_gain * energy / cells_total
    weight = damping / diagonal(0, tension)
    centre, biharm, laplace = stencil(padded)
    rhs_field = load - (mass_term * centre + biharm + tension * laplace)
    update = weight * rhs_field
    leftover = rhs_field - operate(pad_fine(update), 0, tension)
    update = update + prolong(descend(restrict(leftover), 1, tension, pad_fine))
    update = update + weight * (rhs_field - operate(pad_fine(update), 0, tension))
    return predicted + update


def solution(mesh):
    placed = (P("gx", "gy"), P("gx", "gy"), P("gx", "gy"))
    return jax.shard_map(body, mesh=mesh, in_specs=placed, out_specs=P("gx", "gy"), check_vma=False)
```

profile of v0, /device:TPU:0, one launch (start us, length us, event | category | flops | bytes accessed | tf_op | source)
XLA Modules:
  0.0 276.0 jit_solution(13351382852845343121)
XLA Ops:
  1.1 1.3 collective-permute-start
  2.4 3.0 %collective-permute-start.1 = (f32[2,512]{1,0:T(2,128)S(1)}, f32[2,512]{1,0:T(2,128)S(1)}, u32[]{:S(2)}, u32[]{:S(2)}) collective-permute-start(f32[2,512]{1,0:T(2,128)S(1)} %get-tuple-element.38), channel_id=1, source_target_pairs={{0,8},{8,16},{16,24},{1,9},{9,17},{17,25},{2,10},{10,18},{18,26},{... | collective-permute-start | bytes 12296 | tf_op jit(solution)/shard_map/ppermute | solution.py:22
  6.3 1.3 collective-permute-start.2
  7.6 5.5 %collective-permute-start.3 = (f32[132,2]{1,0:T(8,128)S(1)}, f32[132,2]{1,0:T(8,128)S(1)}, u32[]{:S(2)}, u32[]{:S(2)}) collective-permute-start(f32[132,2]{1,0:T(8,128)S(1)} %get-tuple-element.25), channel_id=1, source_target_pairs={{0,1},{1,2},{2,3},{3,4},{4,5},{5,6},{6,7},{8,9},{9,10},{10,11},{11... | collective-permute-start | bytes 3176 | tf_op jit(solution)/shard_map/ppermute | solution.py:22
  13.6 2.5 collective-permute-done.3
  17.0 43.1 %psum.7 = f32[]{:T(128)} all-reduce(f32[]{:T(128)} %add_reduce_fusion), channel_id=1, replica_groups=mesh['gx'=4,'gy'=8] {'gx','gy'}, use_global_device_ids=true, to_apply=%region_1.0 | all-reduce | flops 1 | bytes 8 | tf_op jit(solution)/shard_map/psum | solution.py:126
  60.8 1.5 broadcast_multiply_fusion.1
  63.6 1.3 collective-permute-start.5
  64.9 4.5 %collective-permute-done.5 = f32[2,512]{1,0:T(2,128)S(1)} collective-permute-done((f32[2,512]{1,0:T(2,128)S(1)}, f32[2,512]{1,0:T(2,128)S(1)}, u32[]{:S(2)}, u32[]{:S(2)}) %collective-permute-start.5) | collective-permute-done | bytes 4128 | tf_op jit(solution)/shard_map/ppermute | solution.py:23
  69.5 3.9 %collective-permute-start.6 = (f32[132,2]{1,0:T(8,128)S(1)}, f32[132,2]{1,0:T(8,128)S(1)}, u32[]{:S(2)}, u32[]{:S(2)}) collective-permute-start(f32[132,2]{1,0:T(8,128)S(1)} %get-tuple-element.21), channel_id=1, source_target_pairs={{0,1},{1,2},{2,3},{3,4},{4,5},{5,6},{6,7},{8,9},{9,10},{10,11},{11... | collective-permute-start | bytes 3176 | tf_op jit(solution)/shard_map/ppermute | solution.py:22
  73.4 1.3 collective-permute-start.7
  75.3 4.3 %collective-permute-done.7 = f32[132,2]{1,0:T(8,128)S(1)} collective-permute-done((f32[132,2]{1,0:T(8,128)S(1)}, f32[132,2]{1,0:T(8,128)S(1)}, u32[]{:S(2)}, u32[]{:S(2)}) %collective-permute-start.7) | collective-permute-done | bytes 1088 | tf_op jit(solution)/shard_map/ppermute | solution.py:23
  80.4 18.1 %reshape.27 = f32[64,2,256,2]{3,2,1,0:T(8,128)} reshape(f32[128,512]{1,0:T(8,128)S(1)} %fusion.56) | data formatting | bytes 524288 | tf_op jit(solution)/shard_map/reshape | solution.py:55
  98.4 8.0 %reduce_sum.37 = f32[64,256]{1,0:T(8,128)S(1)} reduce(f32[64,2,256,2]{3,2,1,0:T(8,128)} %reshape.27, f32[]{:T(128)} %constant.36.clone.1), dimensions={1,3}, to_apply=%region_2.0 | reduce | flops 49152 | bytes 327684 | tf_op jit(solution)/shard_map/reduce_sum | solution.py:55
  106.5 2.8 %collective-permute-start.8 = (f32[2,256]{1,0:T(2,128)S(1)}, f32[2,256]{1,0:T(2,128)S(1)}, u32[]{:S(2)}, u32[]{:S(2)}) collective-permute-start(f32[2,256]{1,0:T(2,128)S(1)} %get-tuple-element.65), channel_id=1, source_target_pairs={{0,8},{8,16},{16,24},{1,9},{9,17},{17,25},{2,10},{10,18},{18,26},{... | collective-permute-start | bytes 6152 | tf_op jit(solution)/shard_map/ppermute | solution.py:22
  109.3 1.3 collective-permute-start.9
  110.6 2.7 collective-permute-done.9
  113.4 3.8 %collective-permute-start.10 = (f32[68,2]{1,0:T(8,128)S(1)}, f32[68,2]{1,0:T(8,128)S(1)}, u32[]{:S(2)}, u32[]{:S(2)}) collective-permute-start(f32[68,2]{1,0:T(8,128)S(1)} %get-tuple-element.46), channel_id=1, source_target_pairs={{0,1},{1,2},{2,3},{3,4},{4,5},{5,6},{6,7},{8,9},{9,10},{10,11},{11... | collective-permute-start | bytes 1640 | tf_op jit(solution)/shard_map/ppermute | solution.py:22
  117.2 1.3 collective-permute-start.11
  118.8 4.2 %collective-permute-done.11 = f32[68,2]{1,0:T(8,128)S(1)} collective-permute-done((f32[68,2]{1,0:T(8,128)S(1)}, f32[68,2]{1,0:T(8,128)S(1)}, u32[]{:S(2)}, u32[]{:S(2)}) %collective-permute-start.11) | collective-permute-done | bytes 576 | tf_op jit(solution)/shard_map/ppermute | solution.py:23
  123.4 5.6 %reshape.28 = f32[32,2,128,2]{3,2,1,0:T(8,128)} reshape(f32[64,256]{1,0:T(8,128)S(1)} %fusion.123) | data formatting | bytes 131072 | tf_op jit(solution)/shard_map/reshape | solution.py:55
  129.0 2.8 %reduce_sum.38 = f32[32,128]{1,0:T(8,128)S(1)} reduce(f32[32,2,128,2]{3,2,1,0:T(8,128)} %reshape.28, f32[]{:T(128)} %constant.36.clone.1), dimensions={1,3}, to_apply=%region_3.0 | reduce | flops 12288 | bytes 81924 | tf_op jit(solution)/shard_map/reduce_sum | solution.py:55
  131.8 1.3 collective-permute-start.12
  133.1 1.3 collective-permute-start.13
  134.4 1.3 collective-permute-start.14
  135.7 3.7 %collective-permute-done.13 = f32[32,128]{1,0:T(8,128)S(1)} collective-permute-done((f32[32,128]{1,0:T(8,128)S(1)}, f32[32,128]{1,0:T(8,128)S(1)}, u32[]{:S(2)}, u32[]{:S(2)}) %collective-permute-start.13) | collective-permute-done | bytes 16416 | tf_op jit(solution)/shard_map/ppermute | solution.py:31
  141.9 1.3 collective-permute-start.16
  143.2 1.3 collective-permute-start.17
  144.5 2.2 collective-permute-done.15
  146.7 3.4 %collective-permute-done.16 = f32[128,128]{1,0:T(8,128)S(1)} collective-permute-done((f32[128,128]{1,0:T(8,128)S(1)}, f32[128,128]{1,0:T(8,128)S(1)}, u32[]{:S(2)}, u32[]{:S(2)}) %collective-permute-start.16) | collective-permute-done | bytes 65568 | tf_op jit(solution)/shard_map/ppermute | solution.py:31
  150.1 1.9 collective-permute-done.17
  153.5 6.2 %collective-permute-start.20 = (f32[132,2]{1,0:T(8,128)S(1)}, f32[132,2]{1,0:T(8,128)S(1)}, u32[]{:S(2)}, u32[]{:S(2)}) collective-permute-start(f32[132,2]{1,0:T(8,128)S(1)} %get-tuple-element.17), channel_id=1, source_target_pairs={{0,4},{1,5},{2,6},{3,7},{8,12},{9,13},{10,14},{11,15},{16,20},{17,... | collective-permute-start | bytes 3176 | tf_op jit(solution)/shard_map/ppermute | solution.py:31
  159.8 1.5 collective-permute-start.21
  161.7 5.2 %collective-permute-done.21 = f32[132,2]{1,0:T(8,128)S(1)} collective-permute-done((f32[132,2]{1,0:T(8,128)S(1)}, f32[132,2]{1,0:T(8,128)S(1)}, u32[]{:S(2)}, u32[]{:S(2)}) %collective-permute-start.21) | collective-permute-done | bytes 1088 | tf_op jit(solution)/shard_map/ppermute | solution.py:31
  167.7 18.1 %reshape.29 = f32[64,2,256,2]{3,2,1,0:T(8,128)} reshape(f32[128,512]{1,0:T(8,128)S(1)} %fusion.49) | data formatting | bytes 524288 | tf_op jit(solution)/shard_map/reshape | solution.py:55
  185.8 8.0 %reduce_sum.39 = f32[64,256]{1,0:T(8,128)S(1)} reduce(f32[64,2,256,2]{3,2,1,0:T(8,128)} %reshape.29, f32[]{:T(128)} %constant.36.clone.1), dimensions={1,3}, to_apply=%region_4.0 | reduce | flops 49152 | bytes 327684 | tf_op jit(solution)/shard_map/reduce_sum | solution.py:55
  195.2 1.6 collective-permute-start.24
  196.8 1.3 collective-permute-start.25
  198.4 5.1 %collective-permute-done.25 = f32[68,2]{1,0:T(8,128)S(1)} collective-permute-done((f32[68,2]{1,0:T(8,128)S(1)}, f32[68,2]{1,0:T(8,128)S(1)}, u32[]{:S(2)}, u32[]{:S(2)}) %collective-permute-start.25) | collective-permute-done | bytes 576 | tf_op jit(solution)/shard_map/ppermute | solution.py:31
  205.3 1.6 collective-permute-start.28
  206.9 1.3 collective-permute-start.29
  208.6 5.1 %collective-permute-done.29 = f32[68,2]{1,0:T(8,128)S(1)} collective-permute-done((f32[68,2]{1,0:T(8,128)S(1)}, f32[68,2]{1,0:T(8,128)S(1)}, u32[]{:S(2)}, u32[]{:S(2)}) %collective-permute-start.29) | collective-permute-done | bytes 576 | tf_op jit(solution)/shard_map/ppermute | solution.py:31
  216.0 1.6 collective-permute-start.32
  217.6 1.3 collective-permute-start.33
  219.5 5.2 %collective-permute-done.33 = f32[132,2]{1,0:T(8,128)S(1)} collective-permute-done((f32[132,2]{1,0:T(8,128)S(1)}, f32[132,2]{1,0:T(8,128)S(1)}, u32[]{:S(2)}, u32[]{:S(2)}) %collective-permute-start.33) | collective-permute-done | bytes 1088 | tf_op jit(solution)/shard_map/ppermute | solution.py:31
  225.5 1.3 collective-permute-start.34
  226.8 1.3 collective-permute-start.35
  228.1 1.3 collective-permute-start.36
  230.4 1.6 collective-permute-start.37
  231.9 1.4 collective-permute-start.38
  233.3 3.3 %collective-permute-start.39 = (f32[32,128]{1,0:T(8,128)S(1)}, f32[32,128]{1,0:T(8,128)S(1)}, u32[]{:S(2)}, u32[]{:S(2)}) collective-permute-start(f32[32,128]{1,0:T(8,128)S(1)} %get-tuple-element.58), channel_id=1, source_target_pairs={{0,1},{1,2},{2,3},{3,4},{4,5},{5,6},{6,7},{8,9},{9,10},{10,11},{11... | collective-permute-start | bytes 49160 | tf_op jit(solution)/shard_map/ppermute | solution.py:31
  236.6 1.4 collective-permute-done.39
  239.6 1.3 collective-permute-start.41
  240.9 4.5 %collective-permute-done.41 = f32[2,256]{1,0:T(2,128)S(1)} collective-permute-done((f32[2,256]{1,0:T(2,128)S(1)}, f32[2,256]{1,0:T(2,128)S(1)}, u32[]{:S(2)}, u32[]{:S(2)}) %collective-permute-start.41) | collective-permute-done | bytes 2080 | tf_op jit(solution)/shard_map/ppermute | solution.py:23
  245.5 4.2 %collective-permute-start.42 = (f32[68,2]{1,0:T(8,128)S(1)}, f32[68,2]{1,0:T(8,128)S(1)}, u32[]{:S(2)}, u32[]{:S(2)}) collective-permute-start(f32[68,2]{1,0:T(8,128)S(1)} %get-tuple-element.40), channel_id=1, source_target_pairs={{0,1},{1,2},{2,3},{3,4},{4,5},{5,6},{6,7},{8,9},{9,10},{10,11},{11... | collective-permute-start | bytes 1640 | tf_op jit(solution)/shard_map/ppermute | solution.py:22
  249.7 1.3 collective-permute-start.43
  251.3 4.3 %collective-permute-done.43 = f32[68,2]{1,0:T(8,128)S(1)} collective-permute-done((f32[68,2]{1,0:T(8,128)S(1)}, f32[68,2]{1,0:T(8,128)S(1)}, u32[]{:S(2)}, u32[]{:S(2)}) %collective-permute-start.43) | collective-permute-done | bytes 576 | tf_op jit(solution)/shard_map/ppermute | solution.py:23
  256.5 3.1 %collective-permute-start.44 = (f32[2,512]{1,0:T(2,128)S(1)}, f32[2,512]{1,0:T(2,128)S(1)}, u32[]{:S(2)}, u32[]{:S(2)}) collective-permute-start(f32[2,512]{1,0:T(2,128)S(1)} %get-tuple-element.27), channel_id=1, source_target_pairs={{0,8},{8,16},{16,24},{1,9},{9,17},{17,25},{2,10},{10,18},{18,26},{... | collective-permute-start | bytes 12296 | tf_op jit(solution)/shard_map/ppermute | solution.py:22
  259.6 1.3 collective-permute-start.45
  260.9 2.4 collective-permute-done.45
  263.4 4.8 %collective-permute-start.46 = (f32[132,2]{1,0:T(8,128)S(1)}, f32[132,2]{1,0:T(8,128)S(1)}, u32[]{:S(2)}, u32[]{:S(2)}) collective-permute-start(f32[132,2]{1,0:T(8,128)S(1)} %get-tuple-element.9), channel_id=1, source_target_pairs={{0,1},{1,2},{2,3},{3,4},{4,5},{5,6},{6,7},{8,9},{9,10},{10,11},{11... | collective-permute-start | bytes 3176 | tf_op jit(solution)/shard_map/ppermute | solution.py:22
  268.3 1.3 collective-permute-start.47
  270.2 4.3 %collective-permute-done.47 = f32[132,2]{1,0:T(8,128)S(1)} collective-permute-done((f32[132,2]{1,0:T(8,128)S(1)}, f32[132,2]{1,0:T(8,128)S(1)}, u32[]{:S(2)}, u32[]{:S(2)}) %collective-permute-start.47) | collective-permute-done | bytes 1088 | tf_op jit(solution)/shard_map/ppermute | solution.py:23
  274.7 1.3 fusion.31
  (107 shorter events, 23.8 us)
Async XLA Ops:
  1.1 4.3 %collective-permute-start = (f32[2,512]{1,0:T(2,128)S(1)}, f32[2,512]{1,0:T(2,128)S(1)}, u32[]{:S(2)}, u32[]{:S(2)}) collective-permute-start(f32[2,512]{1,0:T(2,128)S(1)} %get-tuple-element.39), channel_id=1, source_target_pairs={{8,0},{16,8},{24,16},{9,1},{17,9},{25,17},{10,2},{18,10},{26,18},{... | collective-permute-start | bytes 12296 | tf_op jit(solution)/shard_map/ppermute | solution.py:23
  2.4 3.8 %collective-permute-start.1 = (f32[2,512]{1,0:T(2,128)S(1)}, f32[2,512]{1,0:T(2,128)S(1)}, u32[]{:S(2)}, u32[]{:S(2)}) collective-permute-start(f32[2,512]{1,0:T(2,128)S(1)} %get-tuple-element.38), channel_id=1, source_target_pairs={{0,8},{8,16},{16,24},{1,9},{9,17},{17,25},{2,10},{10,18},{18,26},{... | collective-permute-start | bytes 12296 | tf_op jit(solution)/shard_map/ppermute | solution.py:22
  6.3 7.3 %collective-permute-start.2 = (f32[132,2]{1,0:T(8,128)S(1)}, f32[132,2]{1,0:T(8,128)S(1)}, u32[]{:S(2)}, u32[]{:S(2)}) collective-permute-start(f32[132,2]{1,0:T(8,128)S(1)} %get-tuple-element.26), channel_id=1, source_target_pairs={{1,0},{2,1},{3,2},{4,3},{5,4},{6,5},{7,6},{9,8},{10,9},{11,10},{12... | collective-permute-start | bytes 3176 | tf_op jit(solution)/shard_map/ppermute | solution.py:23
  7.6 8.5 %collective-permute-start.3 = (f32[132,2]{1,0:T(8,128)S(1)}, f32[132,2]{1,0:T(8,128)S(1)}, u32[]{:S(2)}, u32[]{:S(2)}) collective-permute-start(f32[132,2]{1,0:T(8,128)S(1)} %get-tuple-element.25), channel_id=1, source_target_pairs={{0,1},{1,2},{2,3},{3,4},{4,5},{5,6},{6,7},{8,9},{9,10},{10,11},{11... | collective-permute-start | bytes 3176 | tf_op jit(solution)/shard_map/ppermute | solution.py:22
  62.3 2.6 collective-permute-start.4
  63.6 5.8 %collective-permute-start.5 = (f32[2,512]{1,0:T(2,128)S(1)}, f32[2,512]{1,0:T(2,128)S(1)}, u32[]{:S(2)}, u32[]{:S(2)}) collective-permute-start(f32[2,512]{1,0:T(2,128)S(1)} %get-tuple-element.37), channel_id=1, source_target_pairs={{8,0},{16,8},{24,16},{9,1},{17,9},{25,17},{10,2},{18,10},{26,18},{... | collective-permute-start | bytes 12296 | tf_op jit(solution)/shard_map/ppermute | solution.py:23
  69.5 5.8 %collective-permute-start.6 = (f32[132,2]{1,0:T(8,128)S(1)}, f32[132,2]{1,0:T(8,128)S(1)}, u32[]{:S(2)}, u32[]{:S(2)}) collective-permute-start(f32[132,2]{1,0:T(8,128)S(1)} %get-tuple-element.21), channel_id=1, source_target_pairs={{0,1},{1,2},{2,3},{3,4},{4,5},{5,6},{6,7},{8,9},{9,10},{10,11},{11... | collective-permute-start | bytes 3176 | tf_op jit(solution)/shard_map/ppermute | solution.py:22
  73.4 6.2 %collective-permute-start.7 = (f32[132,2]{1,0:T(8,128)S(1)}, f32[132,2]{1,0:T(8,128)S(1)}, u32[]{:S(2)}, u32[]{:S(2)}) collective-permute-start(f32[132,2]{1,0:T(8,128)S(1)} %get-tuple-element.22), channel_id=1, source_target_pairs={{1,0},{2,1},{3,2},{4,3},{5,4},{6,5},{7,6},{9,8},{10,9},{11,10},{12... | collective-permute-start | bytes 3176 | tf_op jit(solution)/shard_map/ppermute | solution.py:23
  106.5 4.1 %collective-permute-start.8 = (f32[2,256]{1,0:T(2,128)S(1)}, f32[2,256]{1,0:T(2,128)S(1)}, u32[]{:S(2)}, u32[]{:S(2)}) collective-permute-start(f32[2,256]{1,0:T(2,128)S(1)} %get-tuple-element.65), channel_id=1, source_target_pairs={{0,8},{8,16},{16,24},{1,9},{9,17},{17,25},{2,10},{10,18},{18,26},{... | collective-permute-start | bytes 6152 | tf_op jit(solution)/shard_map/ppermute | solution.py:22
  109.3 4.0 %collective-permute-start.9 = (f32[2,256]{1,0:T(2,128)S(1)}, f32[2,256]{1,0:T(2,128)S(1)}, u32[]{:S(2)}, u32[]{:S(2)}) collective-permute-start(f32[2,256]{1,0:T(2,128)S(1)} %get-tuple-element.66), channel_id=1, source_target_pairs={{8,0},{16,8},{24,16},{9,1},{17,9},{25,17},{10,2},{18,10},{26,18},{... | collective-permute-start | bytes 6152 | tf_op jit(solution)/shard_map/ppermute | solution.py:23
  113.4 5.4 %collective-permute-start.10 = (f32[68,2]{1,0:T(8,128)S(1)}, f32[68,2]{1,0:T(8,128)S(1)}, u32[]{:S(2)}, u32[]{:S(2)}) collective-permute-start(f32[68,2]{1,0:T(8,128)S(1)} %get-tuple-element.46), channel_id=1, source_target_pairs={{0,1},{1,2},{2,3},{3,4},{4,5},{5,6},{6,7},{8,9},{9,10},{10,11},{11... | collective-permute-start | bytes 1640 | tf_op jit(solution)/shard_map/ppermute | solution.py:22
  117.2 5.9 %collective-permute-start.11 = (f32[68,2]{1,0:T(8,128)S(1)}, f32[68,2]{1,0:T(8,128)S(1)}, u32[]{:S(2)}, u32[]{:S(2)}) collective-permute-start(f32[68,2]{1,0:T(8,128)S(1)} %get-tuple-element.47), channel_id=1, source_target_pairs={{1,0},{2,1},{3,2},{4,3},{5,4},{6,5},{7,6},{9,8},{10,9},{11,10},{12... | collective-permute-start | bytes 1640 | tf_op jit(solution)/shard_map/ppermute | solution.py:23
  131.8 3.9 %collective-permute-start.12 = (f32[32,128]{1,0:T(8,128)S(1)}, f32[32,128]{1,0:T(8,128)S(1)}, u32[]{:S(2)}, u32[]{:S(2)}) collective-permute-start(f32[32,128]{1,0:T(8,128)S(1)} %broadcast_multiply_fusion.4), channel_id=1, source_target_pairs={{8,0},{16,8},{24,16},{9,1},{17,9},{25,17},{10,2},{18,10},{26,18},{... | collective-permute-start | bytes 49160 | tf_op jit(solution)/shard_map/ppermute | solution.py:31
  133.1 6.3 %collective-permute-start.13 = (f32[32,128]{1,0:T(8,128)S(1)}, f32[32,128]{1,0:T(8,128)S(1)}, u32[]{:S(2)}, u32[]{:S(2)}) collective-permute-start(f32[32,128]{1,0:T(8,128)S(1)} %broadcast_multiply_fusion.4), channel_id=1, source_target_pairs={{16,0},{24,8},{17,1},{25,9},{18,2},{26,10},{19,3},{27,11},{20,4},{... | collective-permute-start | bytes 49160 | tf_op jit(solution)/shard_map/ppermute | solution.py:31
  134.4 6.2 %collective-permute-start.14 = (f32[32,128]{1,0:T(8,128)S(1)}, f32[32,128]{1,0:T(8,128)S(1)}, u32[]{:S(2)}, u32[]{:S(2)}) collective-permute-start(f32[32,128]{1,0:T(8,128)S(1)} %broadcast_multiply_fusion.4), channel_id=1, source_target_pairs={{24,0},{25,1},{26,2},{27,3},{28,4},{29,5},{30,6},{31,7}} | collective-permute-start | bytes 49160 | tf_op jit(solution)/shard_map/ppermute | solution.py:31
  140.6 6.1 %collective-permute-start.15 = (f32[128,128]{1,0:T(8,128)S(1)}, f32[128,128]{1,0:T(8,128)S(1)}, u32[]{:S(2)}, u32[]{:S(2)}) collective-permute-start(f32[128,128]{1,0:T(8,128)S(1)} %pad_maximum_fusion.47), channel_id=1, source_target_pairs={{1,0},{2,1},{3,2},{4,3},{5,4},{6,5},{7,6},{9,8},{10,9},{11,10},{12... | collective-permute-start | bytes 196616 | tf_op jit(solution)/shard_map/ppermute | solution.py:31
  141.9 8.2 %collective-permute-start.16 = (f32[128,128]{1,0:T(8,128)S(1)}, f32[128,128]{1,0:T(8,128)S(1)}, u32[]{:S(2)}, u32[]{:S(2)}) collective-permute-start(f32[128,128]{1,0:T(8,128)S(1)} %pad_maximum_fusion.47), channel_id=1, source_target_pairs={{2,0},{3,1},{4,2},{5,3},{6,4},{7,5},{10,8},{11,9},{12,10},{13,11},... | collective-permute-start | bytes 196616 | tf_op jit(solution)/shard_map/ppermute | solution.py:31
  143.2 8.9 %collective-permute-start.17 = (f32[128,128]{1,0:T(8,128)S(1)}, f32[128,128]{1,0:T(8,128)S(1)}, u32[]{:S(2)}, u32[]{:S(2)}) collective-permute-start(f32[128,128]{1,0:T(8,128)S(1)} %pad_maximum_fusion.47), channel_id=1, source_target_pairs={{3,0},{4,1},{5,2},{6,3},{7,4},{11,8},{12,9},{13,10},{14,11},{15,12... | collective-permute-start | bytes 196616 | tf_op jit(solution)/shard_map/ppermute | solution.py:31
  152.1 1.3 collective-permute-start.18
  152.8 0.7 collective-permute-start.19
  153.5 8.2 %collective-permute-start.20 = (f32[132,2]{1,0:T(8,128)S(1)}, f32[132,2]{1,0:T(8,128)S(1)}, u32[]{:S(2)}, u32[]{:S(2)}) collective-permute-start(f32[132,2]{1,0:T(8,128)S(1)} %get-tuple-element.17), channel_id=1, source_target_pairs={{0,4},{1,5},{2,6},{3,7},{8,12},{9,13},{10,14},{11,15},{16,20},{17,... | collective-permute-start | bytes 3176 | tf_op jit(solution)/shard_map/ppermute | solution.py:31
  159.8 7.1 %collective-permute-start.21 = (f32[132,2]{1,0:T(8,128)S(1)}, f32[132,2]{1,0:T(8,128)S(1)}, u32[]{:S(2)}, u32[]{:S(2)}) collective-permute-start(f32[132,2]{1,0:T(8,128)S(1)} %get-tuple-element.18), channel_id=1, source_target_pairs={{4,0},{5,1},{6,2},{7,3},{12,8},{13,9},{14,10},{15,11},{20,16},{21,... | collective-permute-start | bytes 3176 | tf_op jit(solution)/shard_map/ppermute | solution.py:31
  193.8 1.3 collective-permute-start.22
  194.5 0.7 collective-permute-start.23
  195.2 3.2 %collective-permute-start.24 = (f32[68,2]{1,0:T(8,128)S(1)}, f32[68,2]{1,0:T(8,128)S(1)}, u32[]{:S(2)}, u32[]{:S(2)}) collective-permute-start(f32[68,2]{1,0:T(8,128)S(1)} %get-tuple-element.44), channel_id=1, source_target_pairs={{0,4},{1,5},{2,6},{3,7},{8,12},{9,13},{10,14},{11,15},{16,20},{17,... | collective-permute-start | bytes 1640 | tf_op jit(solution)/shard_map/ppermute | solution.py:31
  196.8 6.8 %collective-permute-start.25 = (f32[68,2]{1,0:T(8,128)S(1)}, f32[68,2]{1,0:T(8,128)S(1)}, u32[]{:S(2)}, u32[]{:S(2)}) collective-permute-start(f32[68,2]{1,0:T(8,128)S(1)} %get-tuple-element.45), channel_id=1, source_target_pairs={{4,0},{5,1},{6,2},{7,3},{12,8},{13,9},{14,10},{15,11},{20,16},{21,... | collective-permute-start | bytes 1640 | tf_op jit(solution)/shard_map/ppermute | solution.py:31
  203.9 1.3 collective-permute-start.26
  204.5 0.7 collective-permute-start.27
  205.3 3.2 %collective-permute-start.28 = (f32[68,2]{1,0:T(8,128)S(1)}, f32[68,2]{1,0:T(8,128)S(1)}, u32[]{:S(2)}, u32[]{:S(2)}) collective-permute-start(f32[68,2]{1,0:T(8,128)S(1)} %get-tuple-element.42), channel_id=1, source_target_pairs={{0,4},{1,5},{2,6},{3,7},{8,12},{9,13},{10,14},{11,15},{16,20},{17,... | collective-permute-start | bytes 1640 | tf_op jit(solution)/shard_map/ppermute | solution.py:31
  206.9 6.8 %collective-permute-start.29 = (f32[68,2]{1,0:T(8,128)S(1)}, f32[68,2]{1,0:T(8,128)S(1)}, u32[]{:S(2)}, u32[]{:S(2)}) collective-permute-start(f32[68,2]{1,0:T(8,128)S(1)} %get-tuple-element.43), channel_id=1, source_target_pairs={{4,0},{5,1},{6,2},{7,3},{12,8},{13,9},{14,10},{15,11},{20,16},{21,... | collective-permute-start | bytes 1640 | tf_op jit(solution)/shard_map/ppermute | solution.py:31
  214.6 1.3 collective-permute-start.30
  215.2 0.7 collective-permute-start.31
  216.0 3.5 %collective-permute-start.32 = (f32[132,2]{1,0:T(8,128)S(1)}, f32[132,2]{1,0:T(8,128)S(1)}, u32[]{:S(2)}, u32[]{:S(2)}) collective-permute-start(f32[132,2]{1,0:T(8,128)S(1)} %get-tuple-element.13), channel_id=1, source_target_pairs={{0,4},{1,5},{2,6},{3,7},{8,12},{9,13},{10,14},{11,15},{16,20},{17,... | collective-permute-start | bytes 3176 | tf_op jit(solution)/shard_map/ppermute | solution.py:31
  217.6 7.1 %collective-permute-start.33 = (f32[132,2]{1,0:T(8,128)S(1)}, f32[132,2]{1,0:T(8,128)S(1)}, u32[]{:S(2)}, u32[]{:S(2)}) collective-permute-start(f32[132,2]{1,0:T(8,128)S(1)} %get-tuple-element.14), channel_id=1, source_target_pairs={{4,0},{5,1},{6,2},{7,3},{12,8},{13,9},{14,10},{15,11},{20,16},{21,... | collective-permute-start | bytes 3176 | tf_op jit(solution)/shard_map/ppermute | solution.py:31
  225.5 3.9 %collective-permute-start.34 = (f32[32,512]{1,0:T(8,128)S(1)}, f32[32,512]{1,0:T(8,128)S(1)}, u32[]{:S(2)}, u32[]{:S(2)}) collective-permute-start(f32[32,512]{1,0:T(8,128)S(1)} %get-tuple-element.31), channel_id=1, source_target_pairs={{0,24},{1,25},{2,26},{3,27},{4,28},{5,29},{6,30},{7,31}} | collective-permute-start | bytes 196616 | tf_op jit(solution)/shard_map/ppermute | solution.py:31
  226.8 3.5 %collective-permute-start.35 = (f32[32,512]{1,0:T(8,128)S(1)}, f32[32,512]{1,0:T(8,128)S(1)}, u32[]{:S(2)}, u32[]{:S(2)}) collective-permute-start(f32[32,512]{1,0:T(8,128)S(1)} %get-tuple-element.30), channel_id=1, source_target_pairs={{0,16},{8,24},{1,17},{9,25},{2,18},{10,26},{3,19},{11,27},{4,20},{... | collective-permute-start | bytes 196616 | tf_op jit(solution)/shard_map/ppermute | solution.py:31
  228.1 2.2 collective-permute-start.36
  230.4 6.3 %collective-permute-start.37 = (f32[32,128]{1,0:T(8,128)S(1)}, f32[32,128]{1,0:T(8,128)S(1)}, u32[]{:S(2)}, u32[]{:S(2)}) collective-permute-start(f32[32,128]{1,0:T(8,128)S(1)} %get-tuple-element.60), channel_id=1, source_target_pairs={{0,3},{1,4},{2,5},{3,6},{4,7},{8,11},{9,12},{10,13},{11,14},{12,15... | collective-permute-start | bytes 49160 | tf_op jit(solution)/shard_map/ppermute | solution.py:31
  231.9 4.7 %collective-permute-start.38 = (f32[32,128]{1,0:T(8,128)S(1)}, f32[32,128]{1,0:T(8,128)S(1)}, u32[]{:S(2)}, u32[]{:S(2)}) collective-permute-start(f32[32,128]{1,0:T(8,128)S(1)} %get-tuple-element.59), channel_id=1, source_target_pairs={{0,2},{1,3},{2,4},{3,5},{4,6},{5,7},{8,10},{9,11},{10,12},{11,13},... | collective-permute-start | bytes 49160 | tf_op jit(solution)/shard_map/ppermute | solution.py:31
  233.3 4.7 %collective-permute-start.39 = (f32[32,128]{1,0:T(8,128)S(1)}, f32[32,128]{1,0:T(8,128)S(1)}, u32[]{:S(2)}, u32[]{:S(2)}) collective-permute-start(f32[32,128]{1,0:T(8,128)S(1)} %get-tuple-element.58), channel_id=1, source_target_pairs={{0,1},{1,2},{2,3},{3,4},{4,5},{5,6},{6,7},{8,9},{9,10},{10,11},{11... | collective-permute-start | bytes 49160 | tf_op jit(solution)/shard_map/ppermute | solution.py:31
  238.3 2.6 collective-permute-start.40
  239.6 5.8 %collective-permute-start.41 = (f32[2,256]{1,0:T(2,128)S(1)}, f32[2,256]{1,0:T(2,128)S(1)}, u32[]{:S(2)}, u32[]{:S(2)}) collective-permute-start(f32[2,256]{1,0:T(2,128)S(1)} %get-tuple-element.57), channel_id=1, source_target_pairs={{8,0},{16,8},{24,16},{9,1},{17,9},{25,17},{10,2},{18,10},{26,18},{... | collective-permute-start | bytes 6152 | tf_op jit(solution)/shard_map/ppermute | solution.py:23
  245.5 5.8 %collective-permute-start.42 = (f32[68,2]{1,0:T(8,128)S(1)}, f32[68,2]{1,0:T(8,128)S(1)}, u32[]{:S(2)}, u32[]{:S(2)}) collective-permute-start(f32[68,2]{1,0:T(8,128)S(1)} %get-tuple-element.40), channel_id=1, source_target_pairs={{0,1},{1,2},{2,3},{3,4},{4,5},{5,6},{6,7},{8,9},{9,10},{10,11},{11... | collective-permute-start | bytes 1640 | tf_op jit(solution)/shard_map/ppermute | solution.py:22
  249.7 5.9 %collective-permute-start.43 = (f32[68,2]{1,0:T(8,128)S(1)}, f32[68,2]{1,0:T(8,128)S(1)}, u32[]{:S(2)}, u32[]{:S(2)}) collective-permute-start(f32[68,2]{1,0:T(8,128)S(1)} %get-tuple-element.41), channel_id=1, source_target_pairs={{1,0},{2,1},{3,2},{4,3},{5,4},{6,5},{7,6},{9,8},{10,9},{11,10},{12... | collective-permute-start | bytes 1640 | tf_op jit(solution)/shard_map/ppermute | solution.py:23
  256.5 4.4 %collective-permute-start.44 = (f32[2,512]{1,0:T(2,128)S(1)}, f32[2,512]{1,0:T(2,128)S(1)}, u32[]{:S(2)}, u32[]{:S(2)}) collective-permute-start(f32[2,512]{1,0:T(2,128)S(1)} %get-tuple-element.27), channel_id=1, source_target_pairs={{0,8},{8,16},{16,24},{1,9},{9,17},{17,25},{2,10},{10,18},{18,26},{... | collective-permute-start | bytes 12296 | tf_op jit(solution)/shard_map/ppermute | solution.py:22
  259.6 3.8 %collective-permute-start.45 = (f32[2,512]{1,0:T(2,128)S(1)}, f32[2,512]{1,0:T(2,128)S(1)}, u32[]{:S(2)}, u32[]{:S(2)}) collective-permute-start(f32[2,512]{1,0:T(2,128)S(1)} %get-tuple-element.28), channel_id=1, source_target_pairs={{8,0},{16,8},{24,16},{9,1},{17,9},{25,17},{10,2},{18,10},{26,18},{... | collective-permute-start | bytes 12296 | tf_op jit(solution)/shard_map/ppermute | solution.py:23
  263.4 6.8 %collective-permute-start.46 = (f32[132,2]{1,0:T(8,128)S(1)}, f32[132,2]{1,0:T(8,128)S(1)}, u32[]{:S(2)}, u32[]{:S(2)}) collective-permute-start(f32[132,2]{1,0:T(8,128)S(1)} %get-tuple-element.9), channel_id=1, source_target_pairs={{0,1},{1,2},{2,3},{3,4},{4,5},{5,6},{6,7},{8,9},{9,10},{10,11},{11... | collective-permute-start | bytes 3176 | tf_op jit(solution)/shard_map/ppermute | solution.py:22
  268.3 6.2 %collective-permute-start.47 = (f32[132,2]{1,0:T(8,128)S(1)}, f32[132,2]{1,0:T(8,128)S(1)}, u32[]{:S(2)}, u32[]{:S(2)}) collective-permute-start(f32[132,2]{1,0:T(8,128)S(1)} %get-tuple-element.10), channel_id=1, source_target_pairs={{1,0},{2,1},{3,2},{4,3},{5,4},{6,5},{7,6},{9,8},{10,9},{11,10},{12... | collective-permute-start | bytes 3176 | tf_op jit(solution)/shard_map/ppermute | solution.py:23
where the time goes:
time: 278 us; the launch traced here: 276 us
  starting transfers between devices  86.1 us (31%)
  waiting for transfers between devices  73.8 us (27%)
  local copies, waits for them, and re-layouts  43.2 us (16%)
  blocking collectives  43.1 us (16%)
  other arithmetic  27.9 us (10%)
    psum x1, blocking collectives, global_energy(): lax.psum(jnp.sum(down_diff * down_diff + right_diff * right_diff), ('gx',...  43.1 us
    reshape x3, local copies, waits for them, and re-layouts, restrict(): field.reshape(height // 2, 2, breadth // 2, 2).sum(axis=(1, 3))  41.7 us
    ppermute x28, starting transfers between devices, shifted(): lax.ppermute(value, axis, [(source, source + steps) for source in range(l...  39.5 us
    ppermute x28, waiting for transfers between devices, shifted(): lax.ppermute(value, axis, [(source, source + steps) for source in range(l...  37 us
    ppermute x10, starting transfers between devices, extended(): before = lax.ppermute(last, axis, up)  33.7 us
    ppermute x10, waiting for transfers between devices, extended(): after = lax.ppermute(leading, axis, down)  31.7 us
    reduce_sum x3, other arithmetic, restrict(): field.reshape(height // 2, 2, breadth // 2, 2).sum(axis=(1, 3))  18.8 us
    ppermute x10, starting transfers between devices, extended(): after = lax.ppermute(leading, axis, down)  12.9 us
  transfers between devices with their start and end apart: 48, of which 30 were waited for; matrix products, arithmetic and copies ran while one was open for 0% of the time, Pallas kernels for 0%

commit v1 on v0

v1 whole, which is shorter than its diff:
```python
import jax
import jax.numpy as jnp
from jax import lax
from jax.experimental import pallas as pl
from jax.experimental.pallas import tpu as pltpu
from jax.sharding import PartitionSpec as P

COARSE = 3
MASS = 0.0001
DAMPING = 0.5
TENSION_BASE = 1.0
TENSION_GAIN = 3.0

HALO = 64
PAD = 8
LANES = 128
CHUNK = 32
MESH = pl.DeviceIdType.MESH


def near(x):
    rows, cols = x.shape
    across = pltpu.roll(x, 1, 1) + pltpu.roll(x, cols - 1, 1)
    return across + (pltpu.roll(x, 1, 0) + pltpu.roll(x, rows - 1, 0))


def constants(level, tension):
    alpha = 1.0 / 16.0**level
    beta = tension * (1.0 / 4.0**level)
    weight = DAMPING / (MASS + 20.0 * alpha + 4.0 * beta)
    return alpha, beta, weight


def operate(x, alpha, beta):
    y = (4.0 * alpha + beta) * x - alpha * near(x)
    return MASS * x + (4.0 * y - near(y))


def dot2(x, matrix):
    high = x.astype(jnp.bfloat16)
    low = (x - high.astype(jnp.float32)).astype(jnp.bfloat16)
    return jnp.dot(high, matrix, preferred_element_type=jnp.float32) + jnp.dot(
        low, matrix, preferred_element_type=jnp.float32
    )


def halo_parent(lane, width):
    right = lane < width
    left = lane >= LANES - width
    upper = LANES - width // 2 + ((lane - (LANES - width)) >> 1)
    return jnp.where(right, lane >> 1, jnp.where(left, upper, -1))


def last_parent(lane, centre, width):
    halo = lane - centre
    right = centre // 2 + (halo >> 1)
    left = LANES - width // 2 + ((halo - (LANES - width)) >> 1)
    outer = jnp.where(halo < width, right, jnp.where(halo >= LANES - width, left, -1))
    return jnp.where(lane < centre, lane >> 1, outer)


def build(ref, parent, value, transposed):
    fine_dim = 1 if transposed else 0
    fine = lax.broadcasted_iota(jnp.int32, ref.shape, fine_dim)
    coarse = lax.broadcasted_iota(jnp.int32, ref.shape, 1 - fine_dim)
    ref[...] = jnp.where(parent(fine) == coarse, value, 0.0).astype(jnp.bfloat16)


def kernel_body(
    nx, ny, height, breadth,
    d_hbm, v_hbm, load_hbm, out_ref,
    dbuf, vbuf, pbuf, lbuf, lmsg, rmsg, from_right, from_left, edge, abuf, bbuf,
    rtile, etile0, r1t, e1t, r2t, e2t,
    mask1, mask2, mask3,
    c2, ch0, ch1, c3, p2, ph0, ph1, p3,
    part, part2, sums_x, sums_y,
    in_sem, send_sem, recv_sem, red_sem,
):
    gx = lax.axis_index("gx")
    gy = lax.axis_index("gy")
    has_up = gx > 0
    has_down = gx < nx - 1
    has_left = gy > 0
    has_right = gy < ny - 1
    total_rows = height + 2 * HALO
    tiles = breadth // LANES
    width = breadth + LANES

    barrier = pltpu.get_barrier_semaphore()
    for step in range(1, nx):
        pl.semaphore_signal(barrier, 1, device_id=(lax.rem(gx + step, nx), gy), device_id_type=MESH)
    for step in range(1, ny):
        pl.semaphore_signal(barrier, 1, device_id=(gx, lax.rem(gy + step, ny)), device_id_type=MESH)
    diagonals = []
    for dx, okx in ((-1, has_up), (1, has_down)):
        for dy, oky in ((-1, has_left), (1, has_right)):
            ok = jnp.logical_and(okx, oky)
            diagonals.append((dx, dy, ok))

            @pl.when(ok)
            def _(dx=dx, dy=dy):
                pl.semaphore_signal(barrier, 1, device_id=(gx + dx, gy + dy), device_id_type=MESH)

    centre_rows = pl.ds(PAD + HALO, height)
    loads = [
        pltpu.make_async_copy(d_hbm, dbuf, in_sem.at[0]),
        pltpu.make_async_copy(v_hbm, vbuf, in_sem.at[1]),
        pltpu.make_async_copy(load_hbm, lbuf.at[centre_rows, pl.ds(0, breadth)], in_sem.at[2]),
    ]
    for copy in loads:
        copy.start()

    zero_rows = jnp.zeros((PAD, width), jnp.float32)
    for buf in (pbuf, lbuf, abuf, bbuf):
        buf[pl.ds(0, PAD), :] = zero_rows
        buf[pl.ds(PAD + total_rows, PAD), :] = zero_rows

    def clear(ref, start, rows, cols):
        ref[pl.ds(start, rows), pl.ds(0, cols)] = jnp.zeros((rows, cols), jnp.float32)

    @pl.when(jnp.logical_not(has_up))
    def _():
        for buf in (pbuf, lbuf):
            clear(buf, PAD, HALO, breadth)
        clear(from_right, 0, HALO, LANES)
        clear(from_left, 0, HALO, LANES)

    @pl.when(jnp.logical_not(has_down))
    def _():
        for buf in (pbuf, lbuf):
            clear(buf, PAD + HALO + height, HALO, breadth)
        clear(from_right, HALO + height, HALO, LANES)
        clear(from_left, HALO + height, HALO, LANES)
        clear(edge, 0, 8, breadth)

    @pl.when(jnp.logical_not(has_right))
    def _():
        clear(from_right, 0, total_rows, LANES)

    @pl.when(jnp.logical_not(has_left))
    def _():
        clear(from_left, 0, total_rows, LANES)

    loads[0].wait()
    loads[1].wait()
    pbuf[centre_rows, pl.ds(0, breadth)] = dbuf[...] + vbuf[...]
    loads[2].wait()

    lane = lax.broadcasted_iota(jnp.int32, (height, LANES), 1)
    first = lane < HALO
    lmsg[...] = jnp.where(
        first,
        pbuf[centre_rows, pl.ds(0, LANES)],
        pltpu.roll(lbuf[centre_rows, pl.ds(0, LANES)], HALO, 1),
    )
    end = pl.ds(breadth - LANES, LANES)
    rmsg[...] = jnp.where(
        first, pltpu.roll(lbuf[centre_rows, end], HALO, 1), pbuf[centre_rows, end]
    )

    wide = pl.ds(0, breadth)
    top_src = pl.ds(PAD + HALO, HALO)
    bottom_src = pl.ds(PAD + height, HALO)
    top_dst = pl.ds(PAD, HALO)
    bottom_dst = pl.ds(PAD + HALO + height, HALO)
    mid = pl.ds(HALO, height)
    upper, lower = pl.ds(0, HALO), pl.ds(height - HALO, HALO)
    dst_top, dst_bottom = pl.ds(0, HALO), pl.ds(HALO + height, HALO)
    both = jnp.logical_and
    plan = [
        (pbuf.at[pl.ds(PAD + HALO, 8), wide], edge, -1, 0, has_up, has_down),
        (lmsg, from_right.at[mid], 0, -1, has_left, has_right),
        (pbuf.at[top_src, wide], pbuf.at[bottom_dst, wide], -1, 0, has_up, has_down),
        (pbuf.at[bottom_src, wide], pbuf.at[top_dst, wide], 1, 0, has_down, has_up),
        (rmsg, from_left.at[mid], 0, 1, has_right, has_left),
        (lmsg.at[upper], from_right.at[dst_bottom], -1, -1, both(has_up, has_left), both(has_down, has_right)),
        (lmsg.at[lower], from_right.at[dst_top], 1, -1, both(has_down, has_left), both(has_up, has_right)),
        (rmsg.at[upper], from_left.at[dst_bottom], -1, 1, both(has_up, has_right), both(has_down, has_left)),
        (rmsg.at[lower], from_left.at[dst_top], 1, 1, both(has_down, has_right), both(has_up, has_left)),
        (lbuf.at[top_src, wide], lbuf.at[bottom_dst, wide], -1, 0, has_up, has_down),
        (lbuf.at[bottom_src, wide], lbuf.at[top_dst, wide], 1, 0, has_down, has_up),
    ]

    def copy_of(index):
        source, target, dx, dy, _, _ = plan[index]
        return pltpu.make_async_remote_copy(
            src_ref=source,
            dst_ref=target,
            send_sem=send_sem.at[index],
            recv_sem=recv_sem.at[index],
            device_id=(gx + dx, gy + dy),
            device_id_type=MESH,
        )

    def received(index):
        @pl.when(plan[index][5])
        def _():
            copy_of(index).wait_recv()

    count = nx - 1 + ny - 1
    for _, _, ok in diagonals:
        count = count + ok.astype(jnp.int32)
    pl.semaphore_wait(barrier, count)
    for index in range(len(plan)):
        @pl.when(plan[index][4])
        def _(index=index):
            copy_of(index).start()

    x = pbuf[centre_rows, wide]
    row = lax.broadcasted_iota(jnp.int32, (height, breadth), 0)
    col = lax.broadcasted_iota(jnp.int32, (height, breadth), 1)
    down = jnp.where(row < height - 1, pltpu.roll(x, height - 1, 0) - x, 0.0)
    right = jnp.where(col < breadth - 1, pltpu.roll(x, breadth - 1, 1) - x, 0.0)
    inner = jnp.sum(down * down + right * right, axis=0, keepdims=True)
    inner = sum(inner[:, t * LANES : (t + 1) * LANES] for t in range(tiles))

    received(0)
    received(1)
    below = edge[pl.ds(0, 1), :] - x[height - 1 : height, :]
    below = below * below
    below = sum(below[:, t * LANES : (t + 1) * LANES] for t in range(tiles))
    beside = from_right[mid, :] - pltpu.roll(x[:, breadth - LANES :], 1, 1)
    beside = jnp.where(lane == 0, beside * beside, 0.0)
    part[...] = inner + below + jnp.sum(beside, axis=0, keepdims=True)

    def reduce_copy(source, slots, step, axis):
        slot = step - 1
        target = (lax.rem(gx + step, nx), gy) if axis == 0 else (gx, lax.rem(gy + step, ny))
        return pltpu.make_async_remote_copy(
            src_ref=source,
            dst_ref=slots.at[slot],
            send_sem=red_sem.at[axis, 0, slot],
            recv_sem=red_sem.at[axis, 1, slot],
            device_id=target,
            device_id_type=MESH,
        )

    along_x = [reduce_copy(part, sums_x, step, 0) for step in range(1, nx)]
    for copy in along_x:
        copy.start()

    build(c2, lambda i: i >> 1, 0.25, False)
    build(p2, lambda i: i >> 1, 1.0, True)
    build(ch0, lambda i: halo_parent(i, HALO), 0.25, False)
    build(ph0, lambda i: halo_parent(i, HALO), 1.0, True)
    build(ch1, lambda i: halo_parent(i, HALO // 2), 0.25, False)
    build(ph1, lambda i: halo_parent(i, HALO // 2), 1.0, True)
    build(c3, lambda i: last_parent(i, LANES, HALO // 4), 0.25, False)
    build(p3, lambda i: last_parent(i, LANES, HALO // 4), 1.0, True)
    up_f, down_f = has_up.astype(jnp.float32), has_down.astype(jnp.float32)
    left_f, right_f = has_left.astype(jnp.float32), has_right.astype(jnp.float32)

    def lane_mask(cols, centre):
        i = lax.broadcasted_iota(jnp.int32, (1, cols), 1)
        outside = jnp.where(i - centre < (cols - centre) // 2, right_f, left_f)
        return jnp.where(i < centre, 1.0, outside)

    for level, mask in ((1, mask1), (2, mask2), (3, mask3)):
        rim, core = HALO >> level, height >> level
        cols = lane_mask(mask.shape[1], breadth >> level)
        mask[pl.ds(0, rim), :] = jnp.broadcast_to(cols * up_f, (rim, mask.shape[1]))
        mask[pl.ds(rim, core), :] = jnp.broadcast_to(cols, (core, mask.shape[1]))
        mask[pl.ds(rim + core, rim), :] = jnp.broadcast_to(cols * down_f, (rim, mask.shape[1]))

    for copy in along_x:
        copy.wait_recv()
    part2[...] = part[...] + sum(sums_x[i] for i in range(nx - 1))
    along_y = [reduce_copy(part2, sums_y, step, 1) for step in range(1, ny)]
    for copy in along_y:
        copy.start()

    for index in range(2, len(plan)):
        received(index)
    halo_first = lax.broadcasted_iota(jnp.int32, (total_rows, LANES), 1) < HALO
    body_rows = pl.ds(PAD, total_rows)
    outer = pl.ds(breadth, LANES)
    fr, fl = from_right[...], from_left[...]
    pbuf[body_rows, outer] = jnp.where(halo_first, fr, fl)
    lbuf[body_rows, outer] = pltpu.roll(jnp.where(halo_first, fl, fr), HALO, 1)
    fine_mask = lane_mask(width, breadth)

    def prepare(chunk, carry):
        start = pl.multiple_of(chunk * CHUNK, CHUNK)
        x = pbuf[pl.ds(start, CHUNK + 2 * PAD), :]
        s = 4.0 * x - near(x)
        q = 4.0 * s - near(s)
        inside = slice(PAD, PAD + CHUNK)
        rows = pl.ds(pl.multiple_of(start + PAD, 8), CHUNK)
        scale = jnp.where(
            start < HALO, up_f, jnp.where(start >= HALO + height, down_f, 1.0)
        )
        mask = fine_mask * scale
        abuf[rows, :] = (lbuf[rows, :] - MASS * x[inside] - q[inside]) * mask
        bbuf[rows, :] = s[inside] * mask
        return carry

    lax.fori_loop(0, total_rows // CHUNK, prepare, 0)

    for copy in along_y:
        copy.wait_recv()
    energy = jnp.sum(part2[...] + sum(sums_y[i] for i in range(ny - 1)))
    cells = float(height * nx * breadth * ny)
    tension = TENSION_BASE + TENSION_GAIN * energy * (1.0 / cells)

    alpha0, beta0, w0 = constants(0, tension)

    def leave(chunk, carry):
        start = pl.multiple_of(chunk * CHUNK, CHUNK)
        rows = pl.ds(start, CHUNK + 2 * PAD)
        g = abuf[rows, :] - tension * bbuf[rows, :]
        r = (g - w0 * operate(g, alpha0, beta0))[PAD : PAD + CHUNK]
        for t in range(tiles + 1):
            at = pl.multiple_of(t * total_rows + start, 8)
            rtile[pl.ds(at, CHUNK), :] = r[:, t * LANES : (t + 1) * LANES]
        return carry

    lax.fori_loop(0, total_rows // CHUNK, leave, 0)

    def paired(ref, rows, count):
        return [
            ref[pl.ds(t * rows, rows // 2, stride=2), :]
            + ref[pl.ds(t * rows + 1, rows // 2, stride=2), :]
            for t in range(count)
        ]

    def restrict(ref, rows, count, halo_matrix):
        xs = paired(ref, rows, count)
        outs = [
            dot2(jnp.concatenate(xs[t : t + 2], axis=1), c2[...])
            for t in range(0, count - 1, 2)
        ]
        outs.append(dot2(xs[-1], halo_matrix[...]))
        return jnp.concatenate(outs, axis=1)

    def spread(ref, columns, rows):
        for t, x in enumerate(columns):
            ref[pl.ds(t * rows, rows // 2, stride=2), :] = x
            ref[pl.ds(t * rows + 1, rows // 2, stride=2), :] = x

    def prolong(ref, e, rows, halo_matrix):
        count = e.shape[1] // LANES
        columns = []
        for t in range(count - 1):
            pair = dot2(e[:, t * LANES : (t + 1) * LANES], p2[...])
            columns += [pair[:, :LANES], pair[:, LANES:]]
        columns.append(dot2(e[:, (count - 1) * LANES :], halo_matrix[...]))
        spread(ref, columns, rows)

    def gathered(ref, rows, count, first_row, n):
        return jnp.concatenate(
            [ref[pl.ds(t * rows + first_row, n), :] for t in range(count)], axis=1
        )

    def store_tiles(ref, value, rows):
        for t in range(value.shape[1] // LANES):
            ref[pl.ds(t * rows, rows), :] = value[:, t * LANES : (t + 1) * LANES]

    rows1, rows2, rows3 = total_rows // 2, total_rows // 4, total_rows // 8
    count1, count2 = tiles // 2 + 1, tiles // 4 + 1

    g1 = restrict(rtile, total_rows, tiles + 1, ch0) * mask1[...]
    alpha1, beta1, w1 = constants(1, tension)
    store_tiles(r1t, g1 - w1 * operate(g1, alpha1, beta1), rows1)
    g2 = restrict(r1t, rows1, count1, ch1) * mask2[...]
    alpha2, beta2, w2 = constants(2, tension)
    store_tiles(r2t, g2 - w2 * operate(g2, alpha2, beta2), rows2)
    pair = paired(r2t, rows2, count2)
    g3 = dot2(jnp.concatenate(pair, axis=1), c3[...]) * mask3[...]

    alpha3, beta3, w3 = constants(3, tension)
    u3 = w3 * g3
    for _ in range(COARSE - 1):
        u3 = (u3 + w3 * (g3 - operate(u3, alpha3, beta3))) * mask3[...]

    wide_pair = dot2(u3, p3[...])
    spread(e2t, [wide_pair[:, :LANES], wide_pair[:, LANES:]], rows2)
    u2 = w2 * g2 + gathered(e2t, rows2, count2, 0, rows2)
    u2 = (u2 + w2 * (g2 - operate(u2, alpha2, beta2))) * mask2[...]
    prolong(e1t, u2, rows1, ph1)
    u1 = w1 * g1 + gathered(e1t, rows1, count1, 0, rows1)
    u1 = (u1 + w1 * (g1 - operate(u1, alpha1, beta1))) * mask1[...]
    prolong(etile0, u1, total_rows, ph0)

    def finish(chunk, carry):
        start = pl.multiple_of(chunk * CHUNK, CHUNK)
        rows = pl.ds(pl.multiple_of(start + HALO, 8), CHUNK + 2 * PAD)
        g = abuf[rows, :] - tension * bbuf[rows, :]
        e = jnp.concatenate(
            [
                etile0[pl.ds(pl.multiple_of(t * total_rows + start + HALO - PAD, 8), CHUNK + 2 * PAD), :]
                for t in range(tiles + 1)
            ],
            axis=1,
        )
        u = w0 * g + e
        u = (u + w0 * (g - operate(u, alpha0, beta0)))[PAD : PAD + CHUNK, :breadth]
        here = pl.ds(pl.multiple_of(start + HALO + PAD, 8), CHUNK)
        out_ref[pl.ds(start, CHUNK), :] = pbuf[here, wide] + u
        return carry

    lax.fori_loop(0, height // CHUNK, finish, 0)

    for copy in along_x + along_y:
        copy.wait_send()
    for index in range(len(plan)):
        @pl.when(plan[index][4])
        def _(index=index):
            copy_of(index).wait_send()


def body(displacement, velocity, load):
    nx, ny = lax.axis_size("gx"), lax.axis_size("gy")
    height, breadth = displacement.shape
    rows, tiles = height + 2 * HALO, breadth // LANES
    padded = (rows + 2 * PAD, breadth + LANES)
    f32, bf16 = jnp.float32, jnp.bfloat16
    widths = [(breadth >> level) + LANES for level in range(3)] + [LANES]

    def vmem(*shape, dtype=f32):
        return pltpu.VMEM(shape, dtype)

    def tiled(level):
        return vmem(widths[level] // LANES * (rows >> level), LANES)

    scratch = [
        vmem(height, breadth), vmem(height, breadth),
        vmem(*padded), vmem(*padded),
        vmem(height, LANES), vmem(height, LANES),
        vmem(rows, LANES), vmem(rows, LANES),
        vmem(8, breadth), vmem(*padded), vmem(*padded),
        tiled(0), tiled(0), tiled(1), tiled(1), tiled(2), tiled(2),
        vmem(rows // 2, widths[1]), vmem(rows // 4, widths[2]), vmem(rows // 8, widths[3]),
        vmem(2 * LANES, LANES, dtype=bf16), vmem(LANES, LANES, dtype=bf16),
        vmem(LANES, LANES, dtype=bf16), vmem(2 * LANES, LANES, dtype=bf16),
        vmem(LANES, 2 * LANES, dtype=bf16), vmem(LANES, LANES, dtype=bf16),
        vmem(LANES, LANES, dtype=bf16), vmem(LANES, 2 * LANES, dtype=bf16),
        vmem(1, LANES), vmem(1, LANES),
        vmem(nx - 1, 1, LANES), vmem(ny - 1, 1, LANES),
        pltpu.SemaphoreType.DMA((3,)),
        pltpu.SemaphoreType.DMA((11,)),
        pltpu.SemaphoreType.DMA((11,)),
        pltpu.SemaphoreType.DMA((2, 2, max(nx, ny) - 1)),
    ]

    def kernel(*refs):
        kernel_body(nx, ny, height, breadth, *refs)

    return pl.pallas_call(
        kernel,
        out_shape=jax.ShapeDtypeStruct((height, breadth), f32),
        in_specs=[pl.BlockSpec(memory_space=pl.ANY)] * 3,
        out_specs=pl.BlockSpec(memory_space=pltpu.VMEM),
        scratch_shapes=scratch,
        compiler_params=pltpu.CompilerParams(
            collective_id=0, has_side_effects=True, vmem_limit_bytes=32 * 1024 * 1024
        ),
    )(displacement, velocity, load)


def solution(mesh):
    placed = (P("gx", "gy"), P("gx", "gy"), P("gx", "gy"))
    return jax.shard_map(body, mesh=mesh, in_specs=placed, out_specs=P("gx", "gy"), check_vma=False)
```

time: 278 us -> 26.5 us (0.10)
  starting transfers between devices: 86.1 us -> 0 us
  waiting for transfers between devices: 73.8 us -> 0 us
  blocking collectives: 43.1 us -> 0 us
  local copies, waits for them, and re-layouts: 43.2 us -> 3.55 us
  other arithmetic: 27.9 us -> 0 us
  Pallas kernels: 0 us -> 22.7 us
    ppermute x48 -> x0, starting transfers between devices: 86.1 us -> none  [the longest x28 39.5 us: shifted(): lax.ppermute(value, axis, [(source, source + steps) for source in range(l...]
    ppermute x48 -> x0, waiting for transfers between devices: 73.8 us -> none  [the longest x28 37 us: shifted(): lax.ppermute(value, axis, [(source, source + steps) for source in range(l...]
    psum x1 -> x0, blocking collectives: 43.1 us -> none  [global_energy(): lax.psum(jnp.sum(down_diff * down_diff + right_diff * right_diff), ('gx',...]
    reshape x11 -> x0, local copies, waits for them, and re-layouts: 42.5 us -> none  [the longest x3 41.7 us: restrict(): field.reshape(height // 2, 2, breadth // 2, 2).sum(axis=(1, 3))]
    pallas_call x0 -> x1, Pallas kernels: none -> 22.7 us  [body(): pl.pallas_call(kernel, out_shape=jax.ShapeDtypeStruct((height, breadth),...]
    reduce_sum x4 -> x0, other arithmetic: 19.6 us -> none  [the longest x3 18.8 us: restrict(): field.reshape(height // 2, 2, breadth // 2, 2).sum(axis=(1, 3))]
    add x9 -> x0, other arithmetic: 3.66 us -> none  [the longest x1 1.3 us: body(): return predicted + update]
    unnamed x0 -> x7, local copies, waits for them, and re-layouts: none -> 3.55 us
  transfers between devices with their start and end apart: 48 -> 0, of which waited for: 30 -> 0; matrix products, arithmetic and copies ran while one was open for 0% -> 0% of each run, Pallas kernels for 0% -> 0%
where the time goes in v1:
time: 26.5 us; the launch traced here: 26.3 us
  Pallas kernels  22.7 us (86%)
  local copies, waits for them, and re-layouts  3.55 us (13%)
    pallas_call x1, Pallas kernels, body(): pl.pallas_call(kernel, out_shape=jax.ShapeDtypeStruct((height, breadth),...  22.7 us
    unnamed x7, local copies, waits for them, and re-layouts  3.55 us

profile of v1, /device:TPU:0, one launch (start us, length us, event | category | flops | bytes accessed | tf_op | source)
XLA Modules:
  0.0 26.3 jit_solution(12642355584695159837)
XLA Ops:
  0.0 0.0 copy-start
  0.0 0.9 %copy-done = f32[128,512]{1,0:T(8,128)S(1)} copy-done((f32[128,512]{1,0:T(8,128)S(1)}, f32[128,512]{1,0:T(8,128)}, u32[]{:S(2)}) %copy-start) | copy-done | bytes 262168
  1.0 0.0 copy-start.1
  1.0 0.9 %copy-done.1 = f32[128,512]{1,0:T(8,128)S(1)} copy-done((f32[128,512]{1,0:T(8,128)S(1)}, f32[128,512]{1,0:T(8,128)}, u32[]{:S(2)}) %copy-start.1) | copy-done | bytes 262168
  1.9 0.0 copy-start.2
  1.9 0.9 %copy-done.2 = f32[128,512]{1,0:T(8,128)S(1)} copy-done((f32[128,512]{1,0:T(8,128)S(1)}, f32[128,512]{1,0:T(8,128)}, u32[]{:S(2)}) %copy-start.2) | copy-done | bytes 262168
  2.9 22.7 %shard_map.37 = f32[128,512]{1,0:T(8,128)S(1)} custom-call(f32[128,512]{1,0:T(8,128)S(1)} %copy-done, f32[128,512]{1,0:T(8,128)S(1)} %copy-done.1, f32[128,512]{1,0:T(8,128)S(1)} %copy-done.2), custom_call_target="tpu_custom_call" | custom-call | tf_op jit(solution)/shard_map/pallas_call | solution.py:448
  25.6 0.7 %copy.5 = f32[128,512]{1,0:T(8,128)} copy(f32[128,512]{1,0:T(8,128)S(1)} %shard_map.37) | data formatting | bytes 524288
Async XLA Ops:
  0.0 0.9 %copy-start = (f32[128,512]{1,0:T(8,128)S(1)}, f32[128,512]{1,0:T(8,128)}, u32[]{:S(2)}) copy-start(f32[128,512]{1,0:T(8,128)} %refs_0_.1) | copy-start | bytes 786436
  1.0 0.9 %copy-start.1 = (f32[128,512]{1,0:T(8,128)S(1)}, f32[128,512]{1,0:T(8,128)}, u32[]{:S(2)}) copy-start(f32[128,512]{1,0:T(8,128)} %refs_1_.1) | copy-start | bytes 786436
  1.9 0.9 %copy-start.2 = (f32[128,512]{1,0:T(8,128)S(1)}, f32[128,512]{1,0:T(8,128)}, u32[]{:S(2)}) copy-start(f32[128,512]{1,0:T(8,128)} %refs_2_.1) | copy-start | bytes 786436

commit v2 on v1

--- a/solution.py
+++ b/solution.py
@@ -69,11 +69,11 @@
 def kernel_body(
     nx, ny, height, breadth,
     d_hbm, v_hbm, load_hbm, out_ref,
-    dbuf, vbuf, pbuf, lbuf, lmsg, rmsg, from_right, from_left, edge, abuf, bbuf,
+    dbuf, vbuf, pbuf, lbuf, lmsg, rmsg, from_right, from_left, edge, rim, rim_in, abuf, bbuf,
     rtile, etile0, r1t, e1t, r2t, e2t,
     mask1, mask2, mask3,
     c2, ch0, ch1, c3, p2, ph0, ph1, p3,
-    part, part2, sums_x, sums_y,
+    part, sums,
     in_sem, send_sem, recv_sem, red_sem,
 ):
     gx = lax.axis_index("gx")
@@ -87,19 +87,22 @@
     width = breadth + LANES
 
     barrier = pltpu.get_barrier_semaphore()
-    for step in range(1, nx):
-        pl.semaphore_signal(barrier, 1, device_id=(lax.rem(gx + step, nx), gy), device_id_type=MESH)
-    for step in range(1, ny):
-        pl.semaphore_signal(barrier, 1, device_id=(gx, lax.rem(gy + step, ny)), device_id_type=MESH)
-    diagonals = []
-    for dx, okx in ((-1, has_up), (1, has_down)):
-        for dy, oky in ((-1, has_left), (1, has_right)):
-            ok = jnp.logical_and(okx, oky)
-            diagonals.append((dx, dy, ok))
-
-            @pl.when(ok)
-            def _(dx=dx, dy=dy):
-                pl.semaphore_signal(barrier, 1, device_id=(gx + dx, gy + dy), device_id_type=MESH)
+    def every_other(action):
+        for dx in range(nx):
+            ahead = gx + dx
+            tx = jnp.where(ahead >= nx, ahead - nx, ahead)
+
+            def at(dy, carry, dx=dx, tx=tx):
+                along = gy + dy
+                action(dx * ny + dy - 1, (tx, jnp.where(along >= ny, along - ny, along)))
+                return carry
+
+            lax.fori_loop(1 if dx == 0 else 0, ny, at, 0, unroll=ny <= 8)
+
+    def greet(slot, device):
+        pl.semaphore_signal(barrier, 1, device_id=device, device_id_type=MESH)
+
+    every_other(greet)
 
     centre_rows = pl.ds(PAD + HALO, height)
     loads = [
@@ -136,6 +139,7 @@
     @pl.when(jnp.logical_not(has_right))
     def _():
         clear(from_right, 0, total_rows, LANES)
+        clear(rim_in, 0, 8, height)
 
     @pl.when(jnp.logical_not(has_left))
     def _():
@@ -144,6 +148,7 @@
     loads[0].wait()
     loads[1].wait()
     pbuf[centre_rows, pl.ds(0, breadth)] = dbuf[...] + vbuf[...]
+    rim[...] = jnp.transpose(pbuf[centre_rows, pl.ds(0, LANES)])[:8]
     loads[2].wait()
 
     lane = lax.broadcasted_iota(jnp.int32, (height, LANES), 1)
@@ -169,9 +174,10 @@
     both = jnp.logical_and
     plan = [
         (pbuf.at[pl.ds(PAD + HALO, 8), wide], edge, -1, 0, has_up, has_down),
-        (lmsg, from_right.at[mid], 0, -1, has_left, has_right),
+        (rim, rim_in, 0, -1, has_left, has_right),
         (pbuf.at[top_src, wide], pbuf.at[bottom_dst, wide], -1, 0, has_up, has_down),
         (pbuf.at[bottom_src, wide], pbuf.at[top_dst, wide], 1, 0, has_down, has_up),
+        (lmsg, from_right.at[mid], 0, -1, has_left, has_right),
         (rmsg, from_left.at[mid], 0, 1, has_right, has_left),
         (lmsg.at[upper], from_right.at[dst_bottom], -1, -1, both(has_up, has_left), both(has_down, has_right)),
         (lmsg.at[lower], from_right.at[dst_top], 1, -1, both(has_down, has_left), both(has_up, has_right)),
@@ -197,10 +203,7 @@
         def _():
             copy_of(index).wait_recv()
 
-    count = nx - 1 + ny - 1
-    for _, _, ok in diagonals:
-        count = count + ok.astype(jnp.int32)
-    pl.semaphore_wait(barrier, count)
+    pl.semaphore_wait(barrier, nx * ny - 1)
     for index in range(len(plan)):
         @pl.when(plan[index][4])
         def _(index=index):
@@ -214,30 +217,29 @@
     inner = jnp.sum(down * down + right * right, axis=0, keepdims=True)
     inner = sum(inner[:, t * LANES : (t + 1) * LANES] for t in range(tiles))
 
+    last_column = jnp.transpose(x[:, breadth - LANES :])[LANES - 1 :]
+
     received(0)
     received(1)
     below = edge[pl.ds(0, 1), :] - x[height - 1 : height, :]
     below = below * below
     below = sum(below[:, t * LANES : (t + 1) * LANES] for t in range(tiles))
-    beside = from_right[mid, :] - pltpu.roll(x[:, breadth - LANES :], 1, 1)
-    beside = jnp.where(lane == 0, beside * beside, 0.0)
-    part[...] = inner + below + jnp.sum(beside, axis=0, keepdims=True)
-
-    def reduce_copy(source, slots, step, axis):
-        slot = step - 1
-        target = (lax.rem(gx + step, nx), gy) if axis == 0 else (gx, lax.rem(gy + step, ny))
-        return pltpu.make_async_remote_copy(
-            src_ref=source,
-            dst_ref=slots.at[slot],
-            send_sem=red_sem.at[axis, 0, slot],
-            recv_sem=red_sem.at[axis, 1, slot],
-            device_id=target,
+    beside = rim_in[pl.ds(0, 1), :] - last_column
+    beside = beside * beside
+    beside = sum(beside[:, t * LANES : (t + 1) * LANES] for t in range(height // LANES))
+    part[...] = inner + below + beside
+
+    def give(slot, device):
+        pltpu.make_async_remote_copy(
+            src_ref=part,
+            dst_ref=sums.at[slot],
+            send_sem=red_sem.at[0],
+            recv_sem=red_sem.at[1],
+            device_id=device,
             device_id_type=MESH,
-        )
-
-    along_x = [reduce_copy(part, sums_x, step, 0) for step in range(1, nx)]
-    for copy in along_x:
-        copy.start()
+        ).start()
+
+    every_other(give)
 
     build(c2, lambda i: i >> 1, 0.25, False)
     build(p2, lambda i: i >> 1, 1.0, True)
@@ -261,13 +263,6 @@
         mask[pl.ds(0, rim), :] = jnp.broadcast_to(cols * up_f, (rim, mask.shape[1]))
         mask[pl.ds(rim, core), :] = jnp.broadcast_to(cols, (core, mask.shape[1]))
         mask[pl.ds(rim + core, rim), :] = jnp.broadcast_to(cols * down_f, (rim, mask.shape[1]))
-
-    for copy in along_x:
-        copy.wait_recv()
-    part2[...] = part[...] + sum(sums_x[i] for i in range(nx - 1))
-    along_y = [reduce_copy(part2, sums_y, step, 1) for step in range(1, ny)]
-    for copy in along_y:
-        copy.start()
 
     for index in range(2, len(plan)):
         received(index)
@@ -296,9 +291,8 @@
 
     lax.fori_loop(0, total_rows // CHUNK, prepare, 0)
 
-    for copy in along_y:
-        copy.wait_recv()
-    energy = jnp.sum(part2[...] + sum(sums_y[i] for i in range(ny - 1)))
+    pltpu.make_async_copy(sums, sums, red_sem.at[1]).wait()
+    energy = jnp.sum(jnp.sum(sums[...], axis=0) + part[...])
     cells = float(height * nx * breadth * ny)
     tension = TENSION_BASE + TENSION_GAIN * energy * (1.0 / cells)
 
@@ -400,8 +394,7 @@
 
     lax.fori_loop(0, height // CHUNK, finish, 0)
 
-    for copy in along_x + along_y:
-        copy.wait_send()
+    pltpu.make_async_copy(sums, sums, red_sem.at[0]).wait()
     for index in range(len(plan)):
         @pl.when(plan[index][4])
         def _(index=index):
@@ -427,19 +420,19 @@
         vmem(*padded), vmem(*padded),
         vmem(height, LANES), vmem(height, LANES),
         vmem(rows, LANES), vmem(rows, LANES),
-        vmem(8, breadth), vmem(*padded), vmem(*padded),
+        vmem(8, breadth), vmem(8, height), vmem(8, height), vmem(*padded), vmem(*padded),
         tiled(0), tiled(0), tiled(1), tiled(1), tiled(2), tiled(2),
         vmem(rows // 2, widths[1]), vmem(rows // 4, widths[2]), vmem(rows // 8, widths[3]),
         vmem(2 * LANES, LANES, dtype=bf16), vmem(LANES, LANES, dtype=bf16),
         vmem(LANES, LANES, dtype=bf16), vmem(2 * LANES, LANES, dtype=bf16),
         vmem(LANES, 2 * LANES, dtype=bf16), vmem(LANES, LANES, dtype=bf16),
         vmem(LANES, LANES, dtype=bf16), vmem(LANES, 2 * LANES, dtype=bf16),
-        vmem(1, LANES), vmem(1, LANES),
-        vmem(nx - 1, 1, LANES), vmem(ny - 1, 1, LANES),
+        vmem(1, LANES),
+        vmem(nx * ny - 1, 1, LANES),
         pltpu.SemaphoreType.DMA((3,)),
-        pltpu.SemaphoreType.DMA((11,)),
-        pltpu.SemaphoreType.DMA((11,)),
-        pltpu.SemaphoreType.DMA((2, 2, max(nx, ny) - 1)),
+        pltpu.SemaphoreType.DMA((12,)),
+        pltpu.SemaphoreType.DMA((12,)),
+        pltpu.SemaphoreType.DMA((2,)),
     ]
 
     def kernel(*refs):
@@ -448,11 +441,11 @@
     return pl.pallas_call(
         kernel,
         out_shape=jax.ShapeDtypeStruct((height, breadth), f32),
-        in_specs=[pl.BlockSpec(memory_space=pl.ANY)] * 3,
+        in_specs=[pl.BlockSpec(memory_space=pltpu.HBM)] * 3,
         out_specs=pl.BlockSpec(memory_space=pltpu.VMEM),
         scratch_shapes=scratch,
         compiler_params=pltpu.CompilerParams(
-            collective_id=0, has_side_effects=True, vmem_limit_bytes=32 * 1024 * 1024
+            collective_id=0, has_side_effects=True, vmem_limit_bytes=62 * 1024 * 1024
         ),
     )(displacement, velocity, load)
 

time: 26.5 us -> 22.4 us (0.85)
  Pallas kernels: 22.7 us -> 20.5 us
  local copies, waits for them, and re-layouts: 3.55 us -> 1.67 us
    pallas_call x1, Pallas kernels: 22.7 us -> 20.5 us  [body(): pl.pallas_call(kernel, out_shape=jax.ShapeDtypeStruct((height, breadth),...]
    unnamed x7 -> x1, local copies, waits for them, and re-layouts: 3.55 us -> 1.67 us
where the time goes in v2:
time: 22.4 us; the launch traced here: 22.2 us
  Pallas kernels  20.5 us (92%)
  local copies, waits for them, and re-layouts  1.67 us (7%)
    pallas_call x1, Pallas kernels, body(): pl.pallas_call(kernel, out_shape=jax.ShapeDtypeStruct((height, breadth),...  20.5 us
    unnamed x1, local copies, waits for them, and re-layouts  1.67 us

profile of v2, /device:TPU:0, one launch (start us, length us, event | category | flops | bytes accessed | tf_op | source)
XLA Modules:
  0.0 22.2 jit_solution(6029146555555875455)
XLA Ops:
  0.0 20.5 %shard_map.37 = f32[128,512]{1,0:T(8,128)} custom-call(f32[128,512]{1,0:T(8,128)} %refs_0_.1, f32[128,512]{1,0:T(8,128)} %refs_1_.1, f32[128,512]{1,0:T(8,128)} %refs_2_.1), custom_call_target="tpu_custom_call" | custom-call | tf_op jit(solution)/shard_map/pallas_call | solution.py:441
  20.6 1.7 %copy.5 = f32[128,512]{1,0:T(8,128)} copy(f32[128,512]{1,0:T(8,128)} %shard_map.37) | data formatting | bytes 524288

commit v3 on v2

--- a/solution.py
+++ b/solution.py
@@ -14,7 +14,9 @@
 HALO = 64
 PAD = 8
 LANES = 128
-CHUNK = 32
+CHUNK = 64
+DOWN = 256
+UP = 128
 MESH = pl.DeviceIdType.MESH
 
 
@@ -289,7 +291,7 @@
         bbuf[rows, :] = s[inside] * mask
         return carry
 
-    lax.fori_loop(0, total_rows // CHUNK, prepare, 0)
+    lax.fori_loop(0, total_rows // CHUNK, prepare, 0, unroll=True)
 
     pltpu.make_async_copy(sums, sums, red_sem.at[1]).wait()
     energy = jnp.sum(jnp.sum(sums[...], axis=0) + part[...])
@@ -299,16 +301,16 @@
     alpha0, beta0, w0 = constants(0, tension)
 
     def leave(chunk, carry):
-        start = pl.multiple_of(chunk * CHUNK, CHUNK)
-        rows = pl.ds(start, CHUNK + 2 * PAD)
+        start = pl.multiple_of(chunk * DOWN, DOWN)
+        rows = pl.ds(start, DOWN + 2 * PAD)
         g = abuf[rows, :] - tension * bbuf[rows, :]
-        r = (g - w0 * operate(g, alpha0, beta0))[PAD : PAD + CHUNK]
+        r = (g - w0 * operate(g, alpha0, beta0))[PAD : PAD + DOWN]
         for t in range(tiles + 1):
             at = pl.multiple_of(t * total_rows + start, 8)
-            rtile[pl.ds(at, CHUNK), :] = r[:, t * LANES : (t + 1) * LANES]
+            rtile[pl.ds(at, DOWN), :] = r[:, t * LANES : (t + 1) * LANES]
         return carry
 
-    lax.fori_loop(0, total_rows // CHUNK, leave, 0)
+    lax.fori_loop(0, total_rows // DOWN, leave, 0)
 
     def paired(ref, rows, count):
         return [
@@ -376,23 +378,23 @@
     prolong(etile0, u1, total_rows, ph0)
 
     def finish(chunk, carry):
-        start = pl.multiple_of(chunk * CHUNK, CHUNK)
-        rows = pl.ds(pl.multiple_of(start + HALO, 8), CHUNK + 2 * PAD)
+        start = pl.multiple_of(chunk * UP, UP)
+        rows = pl.ds(pl.multiple_of(start + HALO, 8), UP + 2 * PAD)
         g = abuf[rows, :] - tension * bbuf[rows, :]
         e = jnp.concatenate(
             [
-                etile0[pl.ds(pl.multiple_of(t * total_rows + start + HALO - PAD, 8), CHUNK + 2 * PAD), :]
+                etile0[pl.ds(pl.multiple_of(t * total_rows + start + HALO - PAD, 8), UP + 2 * PAD), :]
                 for t in range(tiles + 1)
             ],
             axis=1,
         )
         u = w0 * g + e
-        u = (u + w0 * (g - operate(u, alpha0, beta0)))[PAD : PAD + CHUNK, :breadth]
-        here = pl.ds(pl.multiple_of(start + HALO + PAD, 8), CHUNK)
-        out_ref[pl.ds(start, CHUNK), :] = pbuf[here, wide] + u
+        u = (u + w0 * (g - operate(u, alpha0, beta0)))[PAD : PAD + UP, :breadth]
+        here = pl.ds(pl.multiple_of(start + HALO + PAD, 8), UP)
+        out_ref[pl.ds(start, UP), :] = pbuf[here, wide] + u
         return carry
 
-    lax.fori_loop(0, height // CHUNK, finish, 0)
+    lax.fori_loop(0, height // UP, finish, 0)
 
     pltpu.make_async_copy(sums, sums, red_sem.at[0]).wait()
     for index in range(len(plan)):

time: 22.4 us -> 20.8 us (0.929)
  Pallas kernels: 20.5 us -> 19 us
    pallas_call x1, Pallas kernels: 20.5 us -> 19 us  [body(): pl.pallas_call(kernel, out_shape=jax.ShapeDtypeStruct((height, breadth),...]
where the time goes in v3:
time: 20.8 us; the launch traced here: 20.6 us
  Pallas kernels  19 us (91%)
  local copies, waits for them, and re-layouts  1.67 us (8%)
    pallas_call x1, Pallas kernels, body(): pl.pallas_call(kernel, out_shape=jax.ShapeDtypeStruct((height, breadth),...  19 us
    unnamed x1, local copies, waits for them, and re-layouts  1.67 us

profile of v3, /device:TPU:0, one launch (start us, length us, event | category | flops | bytes accessed | tf_op | source)
XLA Modules:
  0.0 20.6 jit_solution(17245041836823824496)
XLA Ops:
  0.0 19.0 %shard_map.37 = f32[128,512]{1,0:T(8,128)} custom-call(f32[128,512]{1,0:T(8,128)} %refs_0_.1, f32[128,512]{1,0:T(8,128)} %refs_1_.1, f32[128,512]{1,0:T(8,128)} %refs_2_.1), custom_call_target="tpu_custom_call" | custom-call | tf_op jit(solution)/shard_map/pallas_call | solution.py:443
  19.0 1.7 %copy.5 = f32[128,512]{1,0:T(8,128)} copy(f32[128,512]{1,0:T(8,128)} %shard_map.37) | data formatting | bytes 524288
